TPU v7x, 32 devices: a whole 2x2x4 slice. The times are simulated.
32 devices in a mesh: parts: 2 (over x), dp: 2 (over core), mp: 8 (over z, y).
Axes of the slice: x: 2, y: 2, z: 4, core: 2. Of those that a mesh axis runs over, the one named last changes fastest.
Arguments:
- patches: bfloat16 [1024, 6144], P(('parts', 'dp', 'mp')), parts along dimension 0, may hold values from -6 to 6
- norm_gain: float32 [6144], replicated, may hold values from 0.1 to 1.9
- query_gain: float32 [128], replicated, may hold values from 0.5 to 9
- key_gain: float32 [128], replicated, may hold values from 0.5 to 9
- joined_in: bfloat16 [6144, 16, 1536], P(None, ('dp', 'mp')), may hold values from -0.078125 to 0.078125
- joined_out: bfloat16 [16, 1024, 6144], P(('dp', 'mp')), may hold values from -0.046875 to 0.046875
Outputs:
- layer_out: bfloat16 [1024, 6144], P(('parts', 'dp', 'mp')), parts along dimension 0
There are 2 independent parts, one for each index of `parts`. A program takes and returns all parts, laid end to end along the dimension named above; an argument that names none is the same for every part. Nothing has to cross between parts.
All inputs are finite; a program needn't handle non-finite values.
Results may differ from a plain program's by a relative error of at most 0.012.
The roundings to bfloat16 on the way count: a program that leaves them out, or rounds other values in their place, can miss the bound.
Values may be sent and summed in bfloat16 or wider, within the bound.
A program may use at most 128 MiB of HBM per device.

v0:
```python
import jax
import jax.numpy as jnp
from jax import lax
from jax.sharding import PartitionSpec as P

PATCH = 256


def normalize(source, gain):
    values = source.astype(jnp.float32)
    center = values - jnp.mean(values, axis=-1, keepdims=True)
    spread = jnp.mean(center * center, axis=-1, keepdims=True)
    return (center * lax.rsqrt(spread + 1e-06) * gain).astype(jnp.bfloat16)


def attend(joined, query_gain, key_gain, width_att):
    row_count, block_count, _ = joined.shape
    head_dim = query_gain.shape[0]
    heads = block_count * width_att // head_dim
    images = row_count // PATCH
    queries = normalize(joined[:, :, :width_att].reshape(row_count, heads, head_dim), query_gain)
    keys = normalize(
        joined[:, :, width_att : 2 * width_att].reshape(row_count, heads, head_dim), key_gain
    )
    values = (
        joined[:, :, 2 * width_att : 3 * width_att]
        .reshape(row_count, heads, head_dim)
        .astype(jnp.bfloat16)
    )
    queries = queries.reshape(images, PATCH, heads, head_dim)
    keys = keys.reshape(images, PATCH, heads, head_dim)
    values = values.reshape(images, PATCH, heads, head_dim)
    scores = jnp.einsum(
        "iqhd,ikhd->ihqk", queries, keys, preferred_element_type=jnp.float32
    ) * head_dim ** (-0.5)
    largest = jnp.max(scores, axis=-1, keepdims=True)
    raised = jnp.exp(scores - largest)
    weights = (raised / jnp.sum(raised, axis=-1, keepdims=True)).astype(jnp.bfloat16)
    attended = jnp.einsum("ihqk,ikhd->iqhd", weights, values, preferred_element_type=jnp.float32)
    attended = attended.astype(jnp.bfloat16).reshape(row_count, block_count, width_att)
    activated = jax.nn.gelu(joined[:, :, 3 * width_att :], approximate=False).astype(jnp.bfloat16)
    return jnp.concatenate([attended, activated], axis=2)


def shards(patches, norm_gain, query_gain, key_gain, joined_in, joined_out):
    width_mix = joined_out.shape[1]
    block_width = joined_in.shape[2]
    width_att = (block_width - width_mix) // 2
    normed = normalize(patches, norm_gain)
    weight_in = joined_in[:, 0, :]
    weight_out = joined_out[0]
    joined = jnp.dot(
        lax.all_gather(normed, ("dp", "mp"), axis=0, tiled=True),
        weight_in,
        preferred_element_type=jnp.float32,
    )
    mixed = attend(joined.reshape(joined.shape[0], 1, block_width), query_gain, key_gain, width_att)
    flat = mixed.reshape(mixed.shape[0], -1)
    summed = lax.psum_scatter(
        jnp.dot(flat, weight_out, preferred_element_type=jnp.float32),
        ("dp", "mp"),
        scatter_dimension=0,
        tiled=True,
    )
    return (patches.astype(jnp.float32) + summed).astype(jnp.bfloat16)


def solution(mesh):
    in_specs = (
        P(("parts", "dp", "mp"), None),
        P(),
        P(),
        P(),
        P(None, ("dp", "mp"), None),
        P(("dp", "mp"), None, None),
    )
    out_specs = P(("parts", "dp", "mp"), None)
    return jax.shard_map(shards, mesh=mesh, in_specs=in_specs, out_specs=out_specs, check_vma=False)
```

profile of v0, /device:TPU:0, one launch (start us, length us, event | category | flops | bytes accessed | tf_op | source)
XLA Modules:
  0.0 258.9 jit_solution(13603424279514510517)
XLA Ops:
  6.5 1.2 convert_reduce_fusion
  7.7 1.3 fusion.25
  9.0 1.9 fusion.27
  11.0 64.7 %all-gather.2.cloned.1.call-done = bf16[512,6144]{1,0:T(8,128)(2,1)} async-done(((bf16[32,6144]{1,0:T(8,128)(2,1)}), bf16[512,6144]{1,0:T(8,128)(2,1)}) %all-gather.2.cloned.1.call-update) | async-done | bytes 6291472 | tf_op jit(solution)/shard_map/all_gather | solution.py:53
  75.7 14.9 %fusion.5 = f32[512,1,1536]{2,0,1:T(8,128)S(1)} fusion(bf16[512,6144]{1,0:T(8,128)(2,1)} %all-gather.2.cloned.1.call-done, bf16[6144,1,1536]{2,0,1:T(8,128)(2,1)} %param.10), kind=kOutput, calls=%fused_computation.5 | convolution fusion | flops 9663676416 | bytes 28311552 | tf_op jit(solution)/shard_map/dot_general | solution.py:52
  90.6 3.4 %fusion.10 = bf16[512,1,768]{2,0,1:T(8,128)(2,1)S(1)} fusion(f32[512,1,1536]{2,0,1:T(8,128)S(1)} %fusion.5), kind=kLoop, calls=%fused_computation.9 | loop fusion | flops 25559040 | bytes 2359296 | tf_op jit(solution)/shard_map/convert_element_type | solution.py:41
  94.1 0.3 reshape.106
  94.4 0.3 reshape.105
  94.7 0.6 reduce_sum.67
  95.3 1.6 multiply_reduce_fusion
  96.9 0.1 copy.42
  97.0 0.3 reshape.104
  97.3 0.3 reshape.103
  97.6 0.6 reduce_sum.65
  98.3 1.6 multiply_reduce_fusion.1
  99.9 0.1 copy.40
  100.4 0.8 convolution_multiply_fusion
  101.1 0.2 fusion.47
  101.4 0.4 fusion.20
  101.8 0.2 copy.38
  102.0 0.2 reshape.107
  102.2 14.4 %fusion.3 = f32[512,6144]{1,0:T(8,128)} fusion(bf16[1,1024,6144]{2,1,0:T(8,128)(2,1)} %param.11, bf16[512,1,768]{2,0,1:T(8,128)(2,1)S(1)} %fusion.10, bf16[512,1,256]{2,0,1:T(8,128)(2,1)S(1)} %reshape.107), kind=kOutput, calls=%fused_computation.3 | convolution fusion | flops 6444548096 | bytes 26214400 | tf_op jit(solution)/shard_map/dot_general | solution.py:60
  116.6 133.5 %reduce-scatter.2.cloned.1.call-done = f32[32,6144]{1,0:T(8,128)} async-done(((f32[512,6144]{1,0:T(8,128)}), f32[32,6144]{1,0:T(8,128)}) %reduce-scatter.2.cloned.1.call-update) | async-done | bytes 786448 | tf_op jit(solution)/shard_map/reduce_scatter | solution.py:59
  250.1 1.9 fusion.28
  (21 shorter events, 0.6 us)
Async XLA Ops:
  6.5 69.1 %all-gather.2.cloned.1.call-start = ((), (), s32[]{:S(2)}) async-start(), calls=%async_computation.1 | async-start | bytes 6684672 | tf_op jit(solution)/shard_map/all_gather | solution.py:53
  10.9 239.2 %reduce-scatter.2.cloned.1.call-start = ((), (), s32[]{:S(2)}) async-start(), calls=%async_computation.2 | async-start | bytes 13369344 | tf_op jit(solution)/shard_map/reduce_scatter | solution.py:59
  98.2 2.1 copy-start.1
  98.3 2.1 copy-start.2
  116.6 133.5 %copy-start = (bf16[32,6144]{1,0:T(8,128)(2,1)S(1)}, bf16[32,6144]{1,0:T(8,128)(2,1)}, u32[]{:S(2)}) copy-start(bf16[32,6144]{1,0:T(8,128)(2,1)} %param.6) | copy-start | bytes 1179652
Sparse Core Ops, SparseCore 0:
  11.1 64.5 all-gather.1
  116.7 133.3 reduce-scatter.1
where the time goes:
time: 259 us
  waiting for transfers between devices  198 us (76%)
  matrix products  30.5 us (12%)
  other arithmetic  14.6 us (6%)
  between operations  13.6 us (5%)
    reduce_scatter x1, waiting for transfers between devices, shards(): lax.psum_scatter(jnp.dot(flat, weight_out, preferred_element_type=jnp.flo...  134 us
    all_gather x1, waiting for transfers between devices, shards(): lax.all_gather(normed, ('dp', 'mp'), axis=0, tiled=True)  64.7 us
    dot_general x1, matrix products, shards(): jnp.dot(lax.all_gather(normed, ('dp', 'mp'), axis=0, tiled=True), weight_...  14.9 us
    dot_general x1, matrix products, shards(): jnp.dot(flat, weight_out, preferred_element_type=jnp.float32)  14.4 us
  transfers between devices with their start and end apart: 2, of which 2 were waited for; matrix products, arithmetic and copies ran while one was open for 0% of the time, Pallas kernels for 0%

commit v1 on v0

v1 whole, which is shorter than its diff:
```python
import functools

import jax
import jax.numpy as jnp
from jax import lax
from jax.experimental import pallas as pl
from jax.experimental.pallas import tpu as pltpu
from jax.sharding import PartitionSpec as P

PATCH = 256
MESH = pl.DeviceIdType.MESH
Y = 2


def normalize(values, gain):
    center = values - jnp.mean(values, axis=-1, keepdims=True)
    spread = jnp.mean(center * center, axis=-1, keepdims=True)
    return (center * lax.rsqrt(spread + 1e-06) * gain).astype(jnp.bfloat16)


def dot(a, b):
    return jnp.dot(a, b, preferred_element_type=jnp.float32)


def weave(first, second):
    tagged = [((i + 0.5) / len(first), 0, f) for i, f in enumerate(first)]
    tagged += [((i + 0.5) / len(second), 1, f) for i, f in enumerate(second)]
    return [f for _, _, f in sorted(tagged, key=lambda t: t[:2])]


def kernel(
    M, patches, norm_gain, query_gain, key_gain, win_hbm, wout_hbm, out,
    win, wout, xg, joined, mixed, snd, rsib, S, Ry, RZ, fsnd, frecv,
    w_sem, sa_s, sa_r, az_s, az_r, ay_s, ay_r, as_s, as_r,
    ps_s, ps_r, ry_s, ry_r, rz_s, rz_r, f_s, f_r,
):
    R, D = patches.shape
    H = D // 2
    Z = M // Y
    G = M * R
    BW = win.shape[1]
    BW2 = wout.shape[1]
    HD = query_gain.shape[1]
    ATT = (BW - BW2) // 2
    heads = ATT // HD
    NC = snd.shape[1]
    CW = snd.shape[3]
    c = lax.axis_index("dp")
    o = 1 - c
    me = lax.axis_index("mp")
    z = me // Y
    y = me % Y
    yn = z * Y + 1 - y
    drains = []

    def remote(src, dst, ssem, rsem, dev):
        return pltpu.make_async_remote_copy(
            src_ref=src, dst_ref=dst, send_sem=ssem, recv_sem=rsem, device_id=dev, device_id_type=MESH
        )

    def send(cond, make):
        if cond is None:
            make().start()
        else:
            pl.when(cond)(lambda: make().start())
        drains.append((cond, make))

    wcopies = []
    step = D // 4
    for i in range(4):
        wcopies.append(pltpu.make_async_copy(win_hbm.at[pl.ds(i * step, step)], win.at[pl.ds(i * step, step)], w_sem.at[i]))
    for i in range(2):
        wcopies.append(pltpu.make_async_copy(wout_hbm.at[:, pl.ds(i * H, H)], wout.at[i], w_sem.at[4 + i]))
    for w in wcopies:
        w.start()

    barrier = pltpu.get_barrier_semaphore()
    pl.semaphore_signal(barrier, inc=1, device_id={"dp": o}, device_id_type=MESH)
    pl.semaphore_signal(barrier, inc=1, device_id={"mp": yn}, device_id_type=MESH)
    has_dn = z > 0
    has_up = z < Z - 1

    @pl.when(has_dn)
    def _():
        pl.semaphore_signal(barrier, inc=1, device_id={"mp": me - Y}, device_id_type=MESH)

    @pl.when(has_up)
    def _():
        pl.semaphore_signal(barrier, inc=1, device_id={"mp": me + Y}, device_id_type=MESH)

    normed = normalize(patches[...].astype(jnp.float32), norm_gain[...])
    xg[0, c, me] = normed[:, :H]
    xg[1, c, me] = normed[:, H:]
    pl.semaphore_wait(barrier, 2 + (z > 0).astype(jnp.int32) + (z < Z - 1).astype(jnp.int32))

    def own_to_sibling(h):
        return remote(xg.at[h, c, me], xg.at[h, c, me], sa_s.at[h], sa_r.at[h], {"dp": o})

    def own_from_sibling(h):
        return remote(xg.at[h, o, me], xg.at[h, o, me], sa_s.at[h], sa_r.at[h], {"dp": o})

    send(None, lambda: own_to_sibling(o))
    send(None, lambda: own_to_sibling(c))

    def zcopy(g, d, k, b):
        to = me + Y if d == 0 else me - Y
        return remote(xg.at[c, g, b], xg.at[c, g, b], az_s.at[g, d, k], az_r.at[g, d, k], {"mp": to})

    def ycopy(g, zb, b):
        return remote(xg.at[c, g, b], xg.at[c, g, b], ay_s.at[g, zb], ay_r.at[g, zb], {"mp": yn})

    def scopy(g, h, b):
        return remote(xg.at[h, g, b], xg.at[h, g, b], as_s.at[g, b], as_r.at[g, b], {"dp": o})

    def gather_tasks(g):
        tasks = []

        def start():
            @pl.when(c != g)
            def _():
                own_from_sibling(c).wait_recv()
            send(has_up, lambda: zcopy(g, 0, 0, me))
            send(has_dn, lambda: zcopy(g, 1, 0, me))
            send(None, lambda: ycopy(g, z, me))

        tasks.append(start)

        def z_arrival(d, k):
            zb = z - k if d == 0 else z + k
            b = zb * Y + y
            here = z >= k if d == 0 else z + k < Z
            more = jnp.logical_and(here, has_up if d == 0 else has_dn)
            pl.when(here)(lambda: zcopy(g, d, k - 1, b).wait_recv())
            if k < Z - 1:
                send(more, lambda: zcopy(g, d, k, b))
            send(here, lambda: ycopy(g, zb, b))
            send(here, lambda: scopy(g, c, b))

        def y_arrival(d, k):
            zb = z - k if d == 0 else z + k
            b = zb * Y + 1 - y
            here = None if k == 0 else (z >= k if d == 0 else z + k < Z)
            if here is None:
                ycopy(g, zb, b).wait_recv()
            else:
                pl.when(here)(lambda: ycopy(g, zb, b).wait_recv())
            send(here, lambda: scopy(g, c, b))

        for k in range(1, Z):
            for d in (0, 1):
                tasks.append(functools.partial(z_arrival, d, k))
            if k == 1:
                tasks.append(functools.partial(y_arrival, 0, 0))
            else:
                for d in (0, 1):
                    tasks.append(functools.partial(y_arrival, d, k - 1))
        for d in (0, 1):
            tasks.append(functools.partial(y_arrival, d, Z - 1))

        def finish():
            @pl.when(c != g)
            def _():
                own_from_sibling(o).wait_recv()

            @pl.loop(0, M)
            def _(b):
                @pl.when(b != me)
                def _():
                    scopy(g, o, b).wait_recv()

        tasks.append(finish)
        return tasks

    def flat(ref):
        return ref[...].reshape(G, ref.shape[-1])

    NW = 256

    def project(g, first, last):
        @pl.loop(first, last)
        def _(n):
            columns = pl.ds(pl.multiple_of(n * NW, NW), NW)
            left = dot(flat(xg.at[0, g]), win[pl.ds(0, H), columns])
            joined[:, columns] = left + dot(flat(xg.at[1, g]), win[pl.ds(H, H), columns])

    def attention(i, h):
        rows = pl.ds(i * PATCH, PATCH)
        part = lambda at: joined[rows, pl.ds(at * ATT + h * HD, HD)]
        q = normalize(part(0), query_gain[...])
        k = normalize(part(1), key_gain[...])
        v = part(2).astype(jnp.bfloat16)
        scores = lax.dot_general(
            q, k, (((1,), (1,)), ((), ())), preferred_element_type=jnp.float32
        ) * HD ** (-0.5)
        raised = jnp.exp(scores - jnp.max(scores, axis=-1, keepdims=True))
        weights = (raised / jnp.sum(raised, axis=-1, keepdims=True)).astype(jnp.bfloat16)
        mixed[rows, pl.ds(h * HD, HD)] = dot(weights, v).astype(jnp.bfloat16)

    def gelu(n):
        x = joined[:, pl.ds(3 * ATT + n * HD, HD)]
        mixed[:, pl.ds(ATT + n * HD, HD)] = (0.5 * x * (1.0 + lax.erf(x * 0.5**0.5))).astype(jnp.bfloat16)

    def psend(g, n):
        return remote(snd.at[g, n], rsib.at[g, n], ps_s.at[g, n], ps_r.at[g, n], {"dp": o})

    def back_other(g):
        @pl.loop(0, NC)
        def _(n):
            columns = pl.ds(pl.multiple_of(n * CW, CW), CW)
            snd[g, n] = dot(mixed[...], wout[o, :, columns]).astype(jnp.bfloat16)
            psend(g, n).start()

    def back_own(g):
        @pl.loop(0, NC)
        def _(n):
            columns = pl.ds(pl.multiple_of(n * CW, CW), CW)
            term = dot(mixed[...], wout[c, :, columns])
            psend(g, n).wait()
            total = (term + rsib[g, n].astype(jnp.float32)).astype(jnp.bfloat16)
            S[g, :, :, columns] = total.reshape(M, R, CW)

    def compute_tasks(g):
        tasks = []
        chunks = BW // NW
        per = max(1, chunks // 3)
        for a in range(0, chunks, per):
            tasks.append(functools.partial(project, g, a, min(chunks, a + per)))
        for i in range(G // PATCH):
            for h in range(heads):
                tasks.append(functools.partial(attention, i, h))
        units = (BW2 - ATT) // HD
        for n in range(units):
            tasks.append(functools.partial(gelu, n))
        tasks.append(functools.partial(back_other, g))
        tasks.append(functools.partial(back_own, g))
        return tasks

    def ysum(g, zb, b):
        return remote(S.at[g, b], Ry.at[g, zb], ry_s.at[g, zb], ry_r.at[g, zb], {"mp": yn})

    def zsum(g, d, zb):
        to = me + Y if d == 0 else me - Y
        slot = zb if d == 0 else jnp.where(to // Y == zb, Z, zb)
        return remote(S.at[g, zb * Y + y], RZ.at[g, slot], rz_s.at[g, d, zb], rz_r.at[g, d, zb], {"mp": to})

    def zgot(g, d, zb, slot):
        to = me + Y if d == 0 else me - Y
        return remote(RZ.at[g, slot], RZ.at[g, slot], rz_s.at[g, d, zb], rz_r.at[g, d, zb], {"mp": to})

    def scatter_tasks(g):
        tasks = []

        def start():
            order = []
            for j in range((Z + 1) // 2):
                order += [Z - 1 - j] + ([j] if j != Z - 1 - j else [])
            for zb in order:
                send(None, functools.partial(ysum, g, zb, zb * Y + 1 - y))

        tasks.append(start)

        def pass_on(d, j):
            zb = Z - 1 - j if d == 0 else j
            here = zb > z if d == 0 else zb < z
            inner = has_dn if d == 0 else has_up

            @pl.when(here)
            def _():
                at = zb * Y + y
                ysum(g, zb, at).wait_recv()

                @pl.when(inner)
                def _():
                    zgot(g, d, zb, zb).wait_recv()
                    t = S[g, at].astype(jnp.float32) + Ry[g, zb].astype(jnp.float32)
                    S[g, at] = (t + RZ[g, zb].astype(jnp.float32)).astype(jnp.bfloat16)

                @pl.when(jnp.logical_not(inner))
                def _():
                    t = S[g, at].astype(jnp.float32) + Ry[g, zb].astype(jnp.float32)
                    S[g, at] = t.astype(jnp.bfloat16)

            send(here, functools.partial(zsum, g, d, zb))

        for j in range(Z - 1):
            for d in (0, 1):
                tasks.append(functools.partial(pass_on, d, j))

        def finish():
            ysum(g, z, me).wait_recv()
            fsnd[g] = S[g, me].astype(jnp.float32) + Ry[g, z].astype(jnp.float32)

            @pl.when(has_dn)
            def _():
                zgot(g, 0, z, z).wait_recv()
                fsnd[g] += RZ[g, z].astype(jnp.float32)

            @pl.when(has_up)
            def _():
                zgot(g, 1, z, Z).wait_recv()
                fsnd[g] += RZ[g, Z].astype(jnp.float32)

            @pl.when(c == g)
            def _():
                columns = pl.ds(pl.multiple_of(c * H, H), H)
                out[:, columns] = (patches[:, columns].astype(jnp.float32) + fsnd[g]).astype(jnp.bfloat16)

            send(c != g, lambda: remote(fsnd.at[g], frecv, f_s, f_r, {"dp": o}))

        tasks.append(finish)
        return tasks

    def run(tasks):
        for t in tasks:
            t()

    run(gather_tasks(0))
    for w in wcopies:
        w.wait()
    run(weave(gather_tasks(1), compute_tasks(0)))
    run(weave(scatter_tasks(0), compute_tasks(1)))
    run(scatter_tasks(1))
    remote(fsnd.at[0], frecv, f_s, f_r, {"dp": o}).wait_recv()
    columns = pl.ds(pl.multiple_of(o * H, H), H)
    out[:, columns] = (patches[:, columns].astype(jnp.float32) + frecv[...]).astype(jnp.bfloat16)
    for cond, make in drains:
        if cond is None:
            make().wait_send()
        else:
            pl.when(cond)(lambda make=make: make().wait_send())


def shards(M, patches, norm_gain, query_gain, key_gain, joined_in, joined_out):
    R, D = patches.shape
    H = D // 2
    Z = M // Y
    G = M * R
    BW = joined_in.shape[2]
    BW2 = joined_out.shape[1]
    CW = 512
    NC = H // CW
    bf, f32 = jnp.bfloat16, jnp.float32
    V = pl.BlockSpec(memory_space=pltpu.VMEM)
    A = pl.BlockSpec(memory_space=pl.ANY)
    dma = pltpu.SemaphoreType.DMA
    return pl.pallas_call(
        functools.partial(kernel, M),
        out_shape=jax.ShapeDtypeStruct((R, D), bf),
        in_specs=[V, V, V, V, A, A],
        out_specs=V,
        scratch_shapes=[
            pltpu.VMEM((D, BW), bf),
            pltpu.VMEM((2, BW2, H), bf),
            pltpu.VMEM((2, 2, M, R, H), bf),
            pltpu.VMEM((G, BW), f32),
            pltpu.VMEM((G, BW2), bf),
            pltpu.VMEM((2, NC, G, CW), bf),
            pltpu.VMEM((2, NC, G, CW), bf),
            pltpu.VMEM((2, M, R, H), bf),
            pltpu.VMEM((2, Z, R, H), bf),
            pltpu.VMEM((2, Z + 1, R, H), bf),
            pltpu.VMEM((2, R, H), f32),
            pltpu.VMEM((R, H), f32),
            dma((6,)),
            dma((2,)), dma((2,)),
            dma((2, 2, Z)), dma((2, 2, Z)),
            dma((2, Z)), dma((2, Z)),
            dma((2, M)), dma((2, M)),
            dma((2, NC)), dma((2, NC)),
            dma((2, Z)), dma((2, Z)),
            dma((2, 2, Z)), dma((2, 2, Z)),
            dma, dma,
        ],
        compiler_params=pltpu.CompilerParams(
            collective_id=0, has_side_effects=True, vmem_limit_bytes=63 * 1024 * 1024
        ),
        cost_estimate=pl.CostEstimate(
            flops=4 * G * D * (BW + BW2), bytes_accessed=2 * D * (BW + BW2), transcendentals=0
        ),
    )(
        patches,
        norm_gain.reshape(1, -1),
        query_gain.reshape(1, -1),
        key_gain.reshape(1, -1),
        joined_in.reshape(D, BW),
        joined_out.reshape(BW2, D),
    )


def solution(mesh):
    in_specs = (
        P(("parts", "dp", "mp"), None),
        P(),
        P(),
        P(),
        P(None, ("dp", "mp"), None),
        P(("dp", "mp"), None, None),
    )
    out_specs = P(("parts", "dp", "mp"), None)
    body = functools.partial(shards, mesh.shape["mp"])
    return jax.shard_map(body, mesh=mesh, in_specs=in_specs, out_specs=out_specs, check_vma=False)
```

time: 259 us -> 126 us (0.49)
  waiting for transfers between devices: 198 us -> 0 us
  Pallas kernels: 0 us -> 124 us
  matrix products: 30.5 us -> 0 us
  other arithmetic: 14.6 us -> 0 us
  between operations: 13.6 us -> 0.01 us
    reduce_scatter x1 -> x0, waiting for transfers between devices: 134 us -> none  [shards(): lax.psum_scatter(jnp.dot(flat, weight_out, preferred_element_type=jnp.flo...]
    pallas_call x0 -> x1, Pallas kernels: none -> 124 us  [shards(): pl.pallas_call(functools.partial(kernel, M), out_shape=jax.ShapeDtypeStru...]
    all_gather x1 -> x0, waiting for transfers between devices: 64.7 us -> none  [shards(): lax.all_gather(normed, ('dp', 'mp'), axis=0, tiled=True)]
    dot_general x4 -> x0, matrix products: 30.5 us -> none  [the longest x1 14.9 us: shards(): jnp.dot(lax.all_gather(normed, ('dp', 'mp'), axis=0, tiled=True), weight_...]
    convert_element_type x3 -> x0, other arithmetic: 7.32 us -> none  [the longest x1 3.44 us: attend(): jax.nn.gelu(joined[:, :, 3 * width_att:], approximate=False)]
    reduce_sum x6 -> x0, other arithmetic: 6.83 us -> none  [the longest x3 4.46 us: normalize(): spread = jnp.mean(center * center, axis=-1, keepdims=True)]
  transfers between devices with their start and end apart: 2 -> 0, of which waited for: 2 -> 0; matrix products, arithmetic and copies ran while one was open for 0% -> 0% of each run, Pallas kernels for 0% -> 0%
where the time goes in v1:
time: 126 us
  Pallas kernels  124 us (98%)
  local copies, waits for them, and re-layouts  1.77 us (1%)
    pallas_call x1, Pallas kernels, shards(): pl.pallas_call(functools.partial(kernel, M), out_shape=jax.ShapeDtypeStru...  124 us

profile of v1, /device:TPU:0, one launch (start us, length us, event | category | flops | bytes accessed | tf_op | source)
XLA Modules:
  0.0 126.1 jit_solution(12643859400849638918)
XLA Ops:
  0.0 124.4 %shard_map.64 = bf16[32,6144]{1,0:T(8,128)(2,1)} custom-call(bf16[32,6144]{1,0:T(8,128)(2,1)} %patches.1, f32[1,6144]{1,0:T(1,128)} %bitcast.7, f32[1,128]{1,0:T(1,128)} %bitcast.8, f32[1,128]{1,0:T(1,128)} %bitcast.9, bf16[6144,1536]{1,0:T(8,128)(2,1)} %bitcast.5, bf16[1024,6144]{1,0:T(8,128)(2,1)} %bitcast.6), custom_call_target="tpu_custom_call" | custom-call | flops 16106127360 | bytes 31457280 | tf_op jit(solution)/shard_map/pallas_call | solution.py:346
  124.4 1.8 %copy.8 = bf16[32,6144]{1,0:T(8,128)(2,1)} copy(bf16[32,6144]{1,0:T(8,128)(2,1)} %shard_map.64) | data formatting | bytes 786432

commit v2 on v1

--- a/solution.py
+++ b/solution.py
@@ -8,6 +8,7 @@
 from jax.sharding import PartitionSpec as P
 
 PATCH = 256
+FLIGHT = 2
 MESH = pl.DeviceIdType.MESH
 Y = 2
 
@@ -250,18 +251,23 @@
     def scatter_tasks(g):
         tasks = []
 
+        def nth(t):
+            if t == Z - 1:
+                return z
+            return jnp.where(z < Z // 2, Z - 1 - t - (Z - 1 - t <= z).astype(jnp.int32), t + (t >= z).astype(jnp.int32))
+
+        def exchange(t):
+            return ysum(g, nth(t), nth(t) * Y + 1 - y)
+
         def start():
-            order = []
-            for j in range((Z + 1) // 2):
-                order += [Z - 1 - j] + ([j] if j != Z - 1 - j else [])
-            for zb in order:
-                send(None, functools.partial(ysum, g, zb, zb * Y + 1 - y))
+            for t in range(min(FLIGHT, Z)):
+                exchange(t).start()
 
         tasks.append(start)
 
-        def pass_on(d, j):
-            zb = Z - 1 - j if d == 0 else j
-            here = zb > z if d == 0 else zb < z
+        def pass_on(d, t):
+            zb = Z - 1 - t + z if d == 0 else t - (Z - 1 - z)
+            here = t >= z if d == 0 else t >= Z - 1 - z
             inner = has_dn if d == 0 else has_up
 
             @pl.when(here)
@@ -282,9 +288,16 @@
 
             send(here, functools.partial(zsum, g, d, zb))
 
-        for j in range(Z - 1):
+        def advance(t):
+            exchange(t).wait_send()
+            if t + FLIGHT < Z:
+                exchange(t + FLIGHT).start()
+
+        for t in range(Z - 1):
+            tasks.append(functools.partial(advance, t))
             for d in (0, 1):
-                tasks.append(functools.partial(pass_on, d, j))
+                tasks.append(functools.partial(pass_on, d, t))
+        tasks.append(functools.partial(advance, Z - 1))
 
         def finish():
             ysum(g, z, me).wait_recv()
@@ -314,12 +327,16 @@
         for t in tasks:
             t()
 
-    run(gather_tasks(0))
+    first, second = gather_tasks(0), gather_tasks(1)
+    late = 3
+    run(first[:-late] + second[:1] + first[-late:])
     for w in wcopies:
         w.wait()
-    run(weave(gather_tasks(1), compute_tasks(0)))
-    run(weave(scatter_tasks(0), compute_tasks(1)))
-    run(scatter_tasks(1))
+    run(weave(second[1:-late], compute_tasks(0)))
+    lead, trail = scatter_tasks(0), scatter_tasks(1)
+    run(lead[:1] + second[-late:])
+    run(weave(lead[1:-late], compute_tasks(1)))
+    run(trail[:1] + lead[-late:] + trail[1:])
     remote(fsnd.at[0], frecv, f_s, f_r, {"dp": o}).wait_recv()
     columns = pl.ds(pl.multiple_of(o * H, H), H)
     out[:, columns] = (patches[:, columns].astype(jnp.float32) + frecv[...]).astype(jnp.bfloat16)

time: 126 us -> 98.4 us (0.78)
  Pallas kernels: 124 us -> 96.1 us
    pallas_call x1, Pallas kernels: 124 us -> 96.1 us  [shards(): pl.pallas_call(functools.partial(kernel, M), out_shape=jax.ShapeDtypeStru...]
where the time goes in v2:
time: 98.4 us; the launch traced here: 97.8 us
  Pallas kernels  96.1 us (98%)
  local copies, waits for them, and re-layouts  1.77 us (2%)
    pallas_call x1, Pallas kernels, shards(): pl.pallas_call(functools.partial(kernel, M), out_shape=jax.ShapeDtypeStru...  96.1 us

profile of v2, /device:TPU:0, one launch (start us, length us, event | category | flops | bytes accessed | tf_op | source)
XLA Modules:
  0.0 97.8 jit_solution(12585909462903347210)
XLA Ops:
  0.0 96.1 %shard_map.64 = bf16[32,6144]{1,0:T(8,128)(2,1)} custom-call(bf16[32,6144]{1,0:T(8,128)(2,1)} %patches.1, f32[1,6144]{1,0:T(1,128)} %bitcast.7, f32[1,128]{1,0:T(1,128)} %bitcast.8, f32[1,128]{1,0:T(1,128)} %bitcast.9, bf16[6144,1536]{1,0:T(8,128)(2,1)} %bitcast.5, bf16[1024,6144]{1,0:T(8,128)(2,1)} %bitcast.6), custom_call_target="tpu_custom_call" | custom-call | flops 16106127360 | bytes 31457280 | tf_op jit(solution)/shard_map/pallas_call | solution.py:363
  96.1 1.8 %copy.8 = bf16[32,6144]{1,0:T(8,128)(2,1)} copy(bf16[32,6144]{1,0:T(8,128)(2,1)} %shard_map.64) | data formatting | bytes 786432
